TPU v7x, 256 devices: a whole 4x4x8 slice. The times are simulated.
256 devices in a mesh: chan: 64 (over x, z, core), src: 4 (over y).
Axes of the slice: x: 4, y: 4, z: 8, core: 2. Of those that a mesh axis runs over, the one named last changes fastest.
Arguments:
- records: bfloat16 [8192, 4096], P('chan'), may hold values from -600 to 600
- virtual_sources: int32 [64], P('src'), may hold values from 0 to 8191
- pair_group: int32 [32768, 1], P(('chan', 'src')), may hold values from 0 to 63; in each aligned block of 128 rows (0 to 127, 128 to 255, ...) at most 4 rows name the same one
- pair_receiver: int32 [32768], P(('chan', 'src')), may hold values from 0 to 127
- pair_source: int32 [32768], P(('chan', 'src')), may hold values from 0 to 15
- observed: float32 [32768, 2048], P(('chan', 'src')), may hold values from -6 to 6
Outputs:
- adjoint_source: float32 [8192, 4096], P(('chan', 'src'))
- pair_misfit: float32 [32768], P(('chan', 'src'))
Inputs may be any that keep to these rules, and one draw needn't show every extreme that they name: `pair_group`: among the 128 pairs listed by one device at most 4 name the same channel group, and in every draw some device lists exactly 4 pairs for some group.
All inputs are finite; a program needn't handle non-finite values.
Results may differ from a plain program's by a relative error of at most 0.0021.
Values sent between devices are 32-bit elements; how exact they have to be, the bound alone decides.
A program may use at most 64 MiB of HBM per device.

v0:
```python
import math
import jax
import jax.numpy as jnp
from jax import lax
from jax.sharding import PartitionSpec as P

K0 = 64


def fourier_basis(offset, length, time_len, bin_count):
    sample_times = offset + jnp.arange(length, dtype=jnp.int32)[:, None]
    band_bins = K0 + jnp.arange(bin_count, dtype=jnp.int32)[None, :]
    phase_index = band_bins * sample_times % (2 * time_len)
    angles = phase_index.astype(jnp.float32) * (math.pi / time_len)
    return jnp.concatenate([jnp.cos(angles), -jnp.sin(angles)], axis=1)


def forward(signal_rows, bin_count):
    time_len = signal_rows.shape[1]
    block_len = min(512, time_len)

    def add_block(block_index, running):
        offset = block_index * block_len
        segment = lax.dynamic_slice_in_dim(signal_rows, offset, block_len, 1)
        fourier_table = fourier_basis(offset, block_len, time_len, bin_count).astype(jnp.bfloat16)
        return running + jnp.dot(segment, fourier_table, preferred_element_type=jnp.float32)

    return lax.fori_loop(
        0,
        time_len // block_len,
        add_block,
        jnp.zeros((signal_rows.shape[0], 2 * bin_count), jnp.float32),
    )


def inverse(spectral, time_len):
    bin_count = spectral.shape[1] // 2
    block_len = min(512, time_len)

    def fill_block(block_index, output):
        offset = block_index * block_len
        fourier_table = fourier_basis(offset, block_len, time_len, bin_count)
        values = lax.dot_general(
            spectral,
            fourier_table,
            (((1,), (1,)), ((), ())),
            precision=lax.Precision.HIGHEST,
            preferred_element_type=jnp.float32,
        ) * (1.0 / math.sqrt(bin_count))
        return lax.dynamic_update_slice_in_dim(output, values, offset, 1)

    return lax.fori_loop(
        0, time_len // block_len, fill_block, jnp.zeros((spectral.shape[0], time_len), jnp.float32)
    )


def whiten(spectra):
    bin_count = spectra.shape[1] // 2
    band_power = jnp.sum(spectra * spectra, axis=1, keepdims=True) / bin_count
    return spectra / jnp.sqrt(band_power + 1e-06)


def band_taper(bin_count):
    band_bins = jnp.arange(bin_count, dtype=jnp.int32).astype(jnp.float32)
    return 0.5 - 0.5 * jnp.cos((band_bins + 0.5) * (2.0 * math.pi / bin_count))


def pair_terms(source_rows, receiver_rows, observed_rows):
    bin_count = observed_rows.shape[-1] // 2
    weights = band_taper(bin_count)
    source_real = source_rows[..., :bin_count]
    source_imag = source_rows[..., bin_count:]
    receiver_real = receiver_rows[..., :bin_count]
    receiver_imag = receiver_rows[..., bin_count:]
    corr_real = source_real * receiver_real + source_imag * receiver_imag
    corr_imag = source_real * receiver_imag - source_imag * receiver_real
    diff_real = corr_real - observed_rows[..., :bin_count]
    diff_imag = corr_imag - observed_rows[..., bin_count:]
    misfit = jnp.sum(weights * (diff_real * diff_real + diff_imag * diff_imag), axis=-1) / (
        2 * bin_count
    )
    resid_real = weights * diff_real
    resid_imag = weights * diff_imag
    term_real = resid_real * source_real - resid_imag * source_imag
    term_imag = resid_real * source_imag + resid_imag * source_real
    return (misfit, jnp.concatenate([term_real, term_imag], axis=-1))


def per_device(records, virtual_sources, pair_group, pair_receiver, pair_source, observed):
    row_count, time_len = records.shape
    pair_count = observed.shape[0]
    bin_count = observed.shape[1] // 2
    groups = lax.axis_size("chan")
    capacity = 2 * pair_count // groups
    slot_total = groups * capacity
    chan_index = lax.axis_index("chan")
    local_rows = virtual_sources - chan_index * row_count
    inside = (local_rows >= 0) & (local_rows < row_count)
    safe_rows = jnp.clip(local_rows, 0, row_count - 1)
    whitened = whiten(forward(records, bin_count))
    picked = jnp.where(inside[:, None], jnp.take(whitened, safe_rows, axis=0), 0.0)
    sources = lax.psum(picked, "chan")
    destination = pair_group[:, 0]
    group_hits = (destination[:, None] == jnp.arange(groups, dtype=jnp.int32)[None, :]).astype(
        jnp.int32
    )
    slot_ranks = jnp.sum((jnp.cumsum(group_hits, axis=0) - 1) * group_hits, axis=1)
    slot_index = destination * capacity + slot_ranks
    send_receiver = (
        jnp.full((slot_total,), -1, jnp.int32)
        .at[slot_index]
        .set(pair_receiver)
        .reshape(groups, capacity)
    )
    request = lax.all_to_all(send_receiver, "chan", split_axis=0, concat_axis=0, tiled=True)
    found_rows = jnp.take(whitened, jnp.clip(request, 0, row_count - 1), axis=0)
    found_rows = jnp.where((request >= 0)[..., None], found_rows, 0.0)
    fetched = lax.all_to_all(found_rows, "chan", split_axis=0, concat_axis=0, tiled=True)
    receiver_rows = fetched.reshape(slot_total, 2 * bin_count)[slot_index]
    source_rows = jnp.take(sources, pair_source, axis=0)
    pair_misfit, adjoint_term = pair_terms(source_rows, receiver_rows, observed)
    send_terms = (
        jnp.zeros((slot_total, 2 * bin_count), jnp.float32)
        .at[slot_index]
        .set(adjoint_term)
        .reshape(groups, capacity, 2 * bin_count)
    )
    arrived_terms, receivers = (
        lax.all_to_all(send_terms, "chan", split_axis=0, concat_axis=0, tiled=True),
        lax.all_to_all(send_receiver, "chan", split_axis=0, concat_axis=0, tiled=True),
    )
    flat_terms = arrived_terms.reshape(slot_total, 2 * bin_count)
    flat_receivers = receivers.reshape(slot_total)
    selector = (jnp.arange(row_count, dtype=jnp.int32)[:, None] == flat_receivers[None, :]).astype(
        jnp.float32
    )
    adjoint_spectra = jnp.dot(
        selector, flat_terms, precision=lax.Precision.HIGHEST, preferred_element_type=jnp.float32
    )
    adjoint_source = lax.psum_scatter(
        inverse(adjoint_spectra, time_len), "src", scatter_dimension=0, tiled=True
    )
    return (adjoint_source, pair_misfit)


def solution(mesh):
    return jax.shard_map(
        per_device,
        mesh=mesh,
        in_specs=(
            P("chan", None),
            P("src"),
            P(("chan", "src"), None),
            P(("chan", "src")),
            P(("chan", "src")),
            P(("chan", "src"), None),
        ),
        out_specs=(P(("chan", "src"), None), P(("chan", "src"))),
        check_vma=False,
    )
```

profile of v0, /device:TPU:1, one launch (start us, length us, event | category | flops | bytes accessed | tf_op | source)
XLA Modules:
  0.0 526.5 jit_solution(5404071709264893560)
XLA Ops:
  11.4 13.0 %all-to-all-start = ((s32[64,1,4]{2,1,0:T(1,128)}), s32[64,1,4]{2,1,0:T(1,128)S(1)}, u32[]{:S(2)}, u32[]{:S(2)}) async-start(s32[64,1,4]{2,1,0:T(1,128)} %bitcast.4), calls=%async_computation | async-start | bytes 65536 | tf_op jit(solution)/shard_map/all_to_all | solution.py:130
  24.4 85.0 %while.32 = (s32[]{:T(128)}, f32[128,2048]{1,0:T(8,128)S(1)}, bf16[128,4096]{1,0:T(8,128)(2,1)}, s32[]{:T(128)}, s32[]{:T(128)}, /*index=5*/s32[]{:T(128)}, s32[]{:T(128)}) while((s32[]{:T(128)}, f32[128,2048]{1,0:T(8,128)S(1)}, bf16[128,4096]{1,0:T(8,128)(2,1)}, s32[]{:T(128)}, s32[]{:T(128)}, /*index=5*/s32[]{:T(128)}, ...), condition=%wide.region_4.5_spmd.clone, body=%wide.region_3.4_spmd.clone.sunk | while | flops 282068480 | bytes 6434965 | solution.py:28
  24.5 9.0 %cosine_convert_fusion.2 = (bf16[512,1024]{1,0:T(8,128)(2,1)S(1)}, bf16[512,1024]{1,0:T(8,128)(2,1)S(1)}) fusion(s32[512]{0:T(512)S(1)} %iota_add_fusion.10, s32[1024]{0:T(1024)S(1)} %iota_add_fusion.11), kind=kLoop, calls=%fused_computation.39.clone.1 | loop fusion | flops 8912896 | bytes 2103296 | tf_op jit(solution)/shard_map/convert
  35.1 9.0 %cosine_convert_fusion.2 = (bf16[512,1024]{1,0:T(8,128)(2,1)S(1)}, bf16[512,1024]{1,0:T(8,128)(2,1)S(1)}) fusion(s32[512]{0:T(512)S(1)} %iota_add_fusion.10, s32[1024]{0:T(1024)S(1)} %iota_add_fusion.11), kind=kLoop, calls=%fused_computation.39.clone.1 | loop fusion | flops 8912896 | bytes 2103296 | tf_op jit(solution)/shard_map/convert
  45.7 9.0 %cosine_convert_fusion.2 = (bf16[512,1024]{1,0:T(8,128)(2,1)S(1)}, bf16[512,1024]{1,0:T(8,128)(2,1)S(1)}) fusion(s32[512]{0:T(512)S(1)} %iota_add_fusion.10, s32[1024]{0:T(1024)S(1)} %iota_add_fusion.11), kind=kLoop, calls=%fused_computation.39.clone.1 | loop fusion | flops 8912896 | bytes 2103296 | tf_op jit(solution)/shard_map/convert
  56.3 9.0 %cosine_convert_fusion.2 = (bf16[512,1024]{1,0:T(8,128)(2,1)S(1)}, bf16[512,1024]{1,0:T(8,128)(2,1)S(1)}) fusion(s32[512]{0:T(512)S(1)} %iota_add_fusion.10, s32[1024]{0:T(1024)S(1)} %iota_add_fusion.11), kind=kLoop, calls=%fused_computation.39.clone.1 | loop fusion | flops 8912896 | bytes 2103296 | tf_op jit(solution)/shard_map/convert
  67.0 9.0 %cosine_convert_fusion.2 = (bf16[512,1024]{1,0:T(8,128)(2,1)S(1)}, bf16[512,1024]{1,0:T(8,128)(2,1)S(1)}) fusion(s32[512]{0:T(512)S(1)} %iota_add_fusion.10, s32[1024]{0:T(1024)S(1)} %iota_add_fusion.11), kind=kLoop, calls=%fused_computation.39.clone.1 | loop fusion | flops 8912896 | bytes 2103296 | tf_op jit(solution)/shard_map/convert
  77.6 9.0 %cosine_convert_fusion.2 = (bf16[512,1024]{1,0:T(8,128)(2,1)S(1)}, bf16[512,1024]{1,0:T(8,128)(2,1)S(1)}) fusion(s32[512]{0:T(512)S(1)} %iota_add_fusion.10, s32[1024]{0:T(1024)S(1)} %iota_add_fusion.11), kind=kLoop, calls=%fused_computation.39.clone.1 | loop fusion | flops 8912896 | bytes 2103296 | tf_op jit(solution)/shard_map/convert
  88.2 9.0 %cosine_convert_fusion.2 = (bf16[512,1024]{1,0:T(8,128)(2,1)S(1)}, bf16[512,1024]{1,0:T(8,128)(2,1)S(1)}) fusion(s32[512]{0:T(512)S(1)} %iota_add_fusion.10, s32[1024]{0:T(1024)S(1)} %iota_add_fusion.11), kind=kLoop, calls=%fused_computation.39.clone.1 | loop fusion | flops 8912896 | bytes 2103296 | tf_op jit(solution)/shard_map/convert
  98.8 9.0 %cosine_convert_fusion.2 = (bf16[512,1024]{1,0:T(8,128)(2,1)S(1)}, bf16[512,1024]{1,0:T(8,128)(2,1)S(1)}) fusion(s32[512]{0:T(512)S(1)} %iota_add_fusion.10, s32[1024]{0:T(1024)S(1)} %iota_add_fusion.11), kind=kLoop, calls=%fused_computation.39.clone.1 | loop fusion | flops 8912896 | bytes 2103296 | tf_op jit(solution)/shard_map/convert
  114.6 3.6 select_select_fusion
  118.1 10.6 %all-to-all-start.1 = ((f32[64,4,2048]{2,1,0:T(4,128)}), f32[64,4,2048]{2,1,0:T(4,128)}, u32[]{:S(2)}, u32[]{:S(2)}) async-start(f32[64,4,2048]{2,1,0:T(4,128)} %select_select_fusion), calls=%async_computation.1 | async-start | bytes 4194304 | tf_op jit(solution)/shard_map/all_to_all | solution.py:118
  130.4 183.6 %all-reduce.2.cloned.1.call-done = f32[16,2048]{1,0:T(8,128)} async-done(((f32[16,2048]{1,0:T(8,128)}), f32[16,2048]{1,0:T(8,128)}) %all-reduce.2.cloned.1.call-update) | async-done | bytes 131088 | tf_op jit(solution)/shard_map/psum | solution.py:102
  326.0 6.6 %all-to-all-start.2 = ((f32[64,4,2048]{2,1,0:T(4,128)}), f32[64,4,2048]{2,1,0:T(4,128)S(1)}, u32[]{:S(2)}, u32[]{:S(2)}) async-start(f32[64,4,2048]{2,1,0:T(4,128)} %reshape.107), calls=%async_computation.2 | async-start | bytes 4194304 | tf_op jit(solution)/shard_map/all_to_all | solution.py:129
  332.7 51.1 %all-to-all-done.2 = f32[64,4,2048]{2,1,0:T(4,128)S(1)} async-done(((f32[64,4,2048]{2,1,0:T(4,128)}), f32[64,4,2048]{2,1,0:T(4,128)S(1)}, u32[]{:S(2)}, u32[]{:S(2)}) %all-to-all-start.2) | async-done | bytes 2097184 | tf_op jit(solution)/shard_map/all_to_all | solution.py:129
  389.6 101.1 %while.31 = (s32[]{:T(128)}, f32[128,4096]{1,0:T(8,128)}, f32[128,2048]{1,0:T(8,128)S(1)}, s32[]{:T(128)}, s32[]{:T(128)}, /*index=5*/s32[]{:T(128)}, s32[]{:T(128)}) while((s32[]{:T(128)}, f32[128,4096]{1,0:T(8,128)}, f32[128,2048]{1,0:T(8,128)S(1)}, s32[]{:T(128)}, s32[]{:T(128)}, /*index=5*/s32[]{:T(128)}, s32[]{:T(128)}) %tuple.90), condition=%wide.region_9.10_spmd, body=%wide.region_8.9_spmd.sunk | while | flops 1619592704 | bytes 10760323 | solution.py:52
  389.7 8.3 %fusion.46 = (f32[512,1024]{1,0:T(8,128)S(1)}, f32[512,1024]{1,0:T(8,128)S(1)}) fusion(s32[512]{0:T(512)S(1)} %iota_add_fusion.8, s32[1024]{0:T(1024)S(1)} %iota_add_fusion.9), kind=kLoop, calls=%fused_computation.21.clone.1 | loop fusion | flops 7864320 | bytes 4200448 | tf_op jit(solution)/shard_map/while/body/eval_jaxpr/cos | solution.py:15
  398.0 3.4 fusion.47
  402.3 8.3 %fusion.46 = (f32[512,1024]{1,0:T(8,128)S(1)}, f32[512,1024]{1,0:T(8,128)S(1)}) fusion(s32[512]{0:T(512)S(1)} %iota_add_fusion.8, s32[1024]{0:T(1024)S(1)} %iota_add_fusion.9), kind=kLoop, calls=%fused_computation.21.clone.1 | loop fusion | flops 7864320 | bytes 4200448 | tf_op jit(solution)/shard_map/while/body/eval_jaxpr/cos | solution.py:15
  410.6 3.4 fusion.47
  415.0 8.3 %fusion.46 = (f32[512,1024]{1,0:T(8,128)S(1)}, f32[512,1024]{1,0:T(8,128)S(1)}) fusion(s32[512]{0:T(512)S(1)} %iota_add_fusion.8, s32[1024]{0:T(1024)S(1)} %iota_add_fusion.9), kind=kLoop, calls=%fused_computation.21.clone.1 | loop fusion | flops 7864320 | bytes 4200448 | tf_op jit(solution)/shard_map/while/body/eval_jaxpr/cos | solution.py:15
  427.6 8.3 %fusion.46 = (f32[512,1024]{1,0:T(8,128)S(1)}, f32[512,1024]{1,0:T(8,128)S(1)}) fusion(s32[512]{0:T(512)S(1)} %iota_add_fusion.8, s32[1024]{0:T(1024)S(1)} %iota_add_fusion.9), kind=kLoop, calls=%fused_computation.21.clone.1 | loop fusion | flops 7864320 | bytes 4200448 | tf_op jit(solution)/shard_map/while/body/eval_jaxpr/cos | solution.py:15
  435.9 3.4 fusion.47
  440.3 8.3 %fusion.46 = (f32[512,1024]{1,0:T(8,128)S(1)}, f32[512,1024]{1,0:T(8,128)S(1)}) fusion(s32[512]{0:T(512)S(1)} %iota_add_fusion.8, s32[1024]{0:T(1024)S(1)} %iota_add_fusion.9), kind=kLoop, calls=%fused_computation.21.clone.1 | loop fusion | flops 7864320 | bytes 4200448 | tf_op jit(solution)/shard_map/while/body/eval_jaxpr/cos | solution.py:15
  448.6 3.4 fusion.47
  452.9 8.3 %fusion.46 = (f32[512,1024]{1,0:T(8,128)S(1)}, f32[512,1024]{1,0:T(8,128)S(1)}) fusion(s32[512]{0:T(512)S(1)} %iota_add_fusion.8, s32[1024]{0:T(1024)S(1)} %iota_add_fusion.9), kind=kLoop, calls=%fused_computation.21.clone.1 | loop fusion | flops 7864320 | bytes 4200448 | tf_op jit(solution)/shard_map/while/body/eval_jaxpr/cos | solution.py:15
  461.2 3.4 fusion.47
  465.5 8.3 %fusion.46 = (f32[512,1024]{1,0:T(8,128)S(1)}, f32[512,1024]{1,0:T(8,128)S(1)}) fusion(s32[512]{0:T(512)S(1)} %iota_add_fusion.8, s32[1024]{0:T(1024)S(1)} %iota_add_fusion.9), kind=kLoop, calls=%fused_computation.21.clone.1 | loop fusion | flops 7864320 | bytes 4200448 | tf_op jit(solution)/shard_map/while/body/eval_jaxpr/cos | solution.py:15
  473.8 3.4 fusion.47
  478.1 8.3 %fusion.46 = (f32[512,1024]{1,0:T(8,128)S(1)}, f32[512,1024]{1,0:T(8,128)S(1)}) fusion(s32[512]{0:T(512)S(1)} %iota_add_fusion.8, s32[1024]{0:T(1024)S(1)} %iota_add_fusion.9), kind=kLoop, calls=%fused_computation.21.clone.1 | loop fusion | flops 7864320 | bytes 4200448 | tf_op jit(solution)/shard_map/while/body/eval_jaxpr/cos | solution.py:15
  486.5 3.4 fusion.47
  491.3 28.4 %reduce-scatter.2.cloned.1.call-done = f32[32,4096]{1,0:T(8,128)} async-done(((f32[128,4096]{1,0:T(8,128)}), f32[32,4096]{1,0:T(8,128)}) %reduce-scatter.2.cloned.1.call-update) | async-done | bytes 524304 | tf_op jit(solution)/shard_map/reduce_scatter | solution.py:140
  (110 shorter events, 52.1 us)
Async XLA Ops:
  11.4 98.4 %all-to-all-start = ((s32[64,1,4]{2,1,0:T(1,128)}), s32[64,1,4]{2,1,0:T(1,128)S(1)}, u32[]{:S(2)}, u32[]{:S(2)}) async-start(s32[64,1,4]{2,1,0:T(1,128)} %bitcast.4), calls=%async_computation | async-start | bytes 65536 | tf_op jit(solution)/shard_map/all_to_all | solution.py:130
  118.1 10.7 %copy-start = (s32[16]{0:T(128)S(1)}, s32[16]{0:T(128)}, u32[]{:S(2)}) copy-start(s32[16]{0:T(128)} %param.11) | copy-start | bytes 196
  118.1 12.2 %copy-start.1 = (s32[128]{0:T(128)S(1)}, s32[128]{0:T(128)}, u32[]{:S(2)}) copy-start(s32[128]{0:T(128)} %param.14) | copy-start | bytes 1540
  118.1 198.3 %all-to-all-start.1 = ((f32[64,4,2048]{2,1,0:T(4,128)}), f32[64,4,2048]{2,1,0:T(4,128)}, u32[]{:S(2)}, u32[]{:S(2)}) async-start(f32[64,4,2048]{2,1,0:T(4,128)} %select_select_fusion), calls=%async_computation.1 | async-start | bytes 4194304 | tf_op jit(solution)/shard_map/all_to_all | solution.py:118
  128.8 185.2 %all-reduce.2.cloned.1.call-start = ((), (), s32[]{:S(2)}) async-start(), calls=%async_computation.4 | async-start | bytes 262144 | tf_op jit(solution)/shard_map/psum | solution.py:102
  326.0 57.9 %all-to-all-start.2 = ((f32[64,4,2048]{2,1,0:T(4,128)}), f32[64,4,2048]{2,1,0:T(4,128)S(1)}, u32[]{:S(2)}, u32[]{:S(2)}) async-start(f32[64,4,2048]{2,1,0:T(4,128)} %reshape.107), calls=%async_computation.2 | async-start | bytes 4194304 | tf_op jit(solution)/shard_map/all_to_all | solution.py:129
  332.6 187.1 %reduce-scatter.2.cloned.1.call-start = ((), (), s32[]{:S(2)}) async-start(), calls=%async_computation.5 | async-start | bytes 2621440 | tf_op jit(solution)/shard_map/reduce_scatter | solution.py:140
Sparse Core Ops, SparseCore 0:
  133.7 180.2 all-reduce.1
  490.9 28.7 reduce-scatter.1
where the time goes:
time: 527 us
  waiting for transfers between devices  263 us (50%)
  other arithmetic  151 us (29%)
  matrix products  42.2 us (8%)
  starting transfers between devices  30.3 us (6%)
  local copies, waits for them, and re-layouts  24.8 us (5%)
  between operations  14.3 us (3%)
    psum x1, waiting for transfers between devices, per_device(): sources = lax.psum(picked, 'chan')  184 us
    another operation x8, other arithmetic  72.2 us
    cos x8, other arithmetic, fourier_basis(): return jnp.concatenate([jnp.cos(angles), -jnp.sin(angles)], axis=1)  66.4 us
    all_to_all x1, waiting for transfers between devices, per_device(): lax.all_to_all(send_terms, 'chan', split_axis=0, concat_axis=0, tiled=True)  51.1 us
    reduce_scatter x1, waiting for transfers between devices, per_device(): lax.psum_scatter(inverse(adjoint_spectra, time_len), 'src', scatter_dimen...  28.4 us
    dot_general x8, matrix products, fill_block(): lax.dot_general(spectral, fourier_table, (((1,), (1,)), ((), ())), precis...  27.4 us
    all_to_all x1, starting transfers between devices, per_device(): lax.all_to_all(send_receiver, 'chan', split_axis=0, concat_axis=0, tiled=...  13 us
    dot_general x8, matrix products, add_block(): jnp.dot(segment, fourier_table, preferred_element_type=jnp.float32)  12.3 us
  transfers between devices with their start and end apart: 5, of which 3 were waited for; matrix products, arithmetic and copies ran while one was open for 17% of the time, Pallas kernels for 0%

commit v1 on v0

--- a/solution.py
+++ b/solution.py
@@ -99,7 +99,7 @@
     safe_rows = jnp.clip(local_rows, 0, row_count - 1)
     whitened = whiten(forward(records, bin_count))
     picked = jnp.where(inside[:, None], jnp.take(whitened, safe_rows, axis=0), 0.0)
-    sources = lax.psum(picked, "chan")
+    sources = jnp.sum(lax.all_gather(picked, "chan"), axis=0)
     destination = pair_group[:, 0]
     group_hits = (destination[:, None] == jnp.arange(groups, dtype=jnp.int32)[None, :]).astype(
         jnp.int32

time: 527 us -> 417 us (0.79)
  waiting for transfers between devices: 263 us -> 148 us
  blocking collectives: 0 us -> 22.1 us
  starting transfers between devices: 30.3 us -> 14 us
    psum x1 -> x0, waiting for transfers between devices: 184 us -> none  [per_device(): sources = lax.psum(picked, 'chan')]
    all_to_all x1, waiting for transfers between devices: 0.01 us -> 65 us  [per_device(): lax.all_to_all(found_rows, 'chan', split_axis=0, concat_axis=0, tiled=True)]
    all_to_all x0 -> x1, blocking collectives: none -> 22.1 us  [per_device(): lax.all_to_all(send_receiver, 'chan', split_axis=0, concat_axis=0, tiled=...]
    all_to_all x1 -> x0, starting transfers between devices: 13 us -> none  [per_device(): lax.all_to_all(send_receiver, 'chan', split_axis=0, concat_axis=0, tiled=...]
  transfers between devices with their start and end apart: 5 -> 4, of which waited for: 3 -> 4; matrix products, arithmetic and copies ran while one was open for 17% -> 3% of each run, Pallas kernels for 0% -> 0%
where the time goes in v1:
time: 417 us; the launch traced here: 416 us
  other arithmetic  152 us (36%)
  waiting for transfers between devices  148 us (35%)
  matrix products  41.9 us (10%)
  local copies, waits for them, and re-layouts  23.2 us (6%)
  blocking collectives  22.1 us (5%)
  between operations  14.3 us (3%)
  starting transfers between devices  14 us (3%)
    another operation x8, other arithmetic  72.2 us
    cos x8, other arithmetic, fourier_basis(): return jnp.concatenate([jnp.cos(angles), -jnp.sin(angles)], axis=1)  66.4 us
    all_to_all x1, waiting for transfers between devices, per_device(): lax.all_to_all(found_rows, 'chan', split_axis=0, concat_axis=0, tiled=True)  65 us
    all_to_all x1, waiting for transfers between devices, per_device(): lax.all_to_all(send_terms, 'chan', split_axis=0, concat_axis=0, tiled=True)  51.1 us
    reduce_scatter x1, waiting for transfers between devices, per_device(): lax.psum_scatter(inverse(adjoint_spectra, time_len), 'src', scatter_dimen...  28.6 us
    dot_general x8, matrix products, fill_block(): lax.dot_general(spectral, fourier_table, (((1,), (1,)), ((), ())), precis...  27.4 us
    all_to_all x1, blocking collectives, per_device(): lax.all_to_all(send_receiver, 'chan', split_axis=0, concat_axis=0, tiled=...  22.1 us
    dot_general x8, matrix products, add_block(): jnp.dot(segment, fourier_table, preferred_element_type=jnp.float32)  12 us
  transfers between devices with their start and end apart: 4, of which 4 were waited for; matrix products, arithmetic and copies ran while one was open for 3% of the time, Pallas kernels for 0%

profile of v1, /device:TPU:1, one launch (start us, length us, event | category | flops | bytes accessed | tf_op | source)
XLA Modules:
  0.0 415.8 jit_solution(9492120250500539356)
XLA Ops:
  7.2 84.7 %while.32 = (s32[]{:T(128)}, f32[128,2048]{1,0:T(8,128)S(1)}, bf16[128,4096]{1,0:T(8,128)(2,1)}, s32[]{:T(128)}, s32[]{:T(128)}, /*index=5*/s32[]{:T(128)}, s32[]{:T(128)}) while((s32[]{:T(128)}, f32[128,2048]{1,0:T(8,128)S(1)}, bf16[128,4096]{1,0:T(8,128)(2,1)}, s32[]{:T(128)}, s32[]{:T(128)}, /*index=5*/s32[]{:T(128)}, ...), condition=%wide.region_4.5_spmd.clone, body=%wide.region_3.4_spmd.clone.sunk | while | flops 282068480 | bytes 6434957 | solution.py:28
  7.3 9.0 %cosine_convert_fusion.2 = (bf16[512,1024]{1,0:T(8,128)(2,1)S(1)}, bf16[512,1024]{1,0:T(8,128)(2,1)S(1)}) fusion(s32[512]{0:T(512)S(1)} %iota_add_fusion.10, s32[1024]{0:T(1024)S(1)} %iota_add_fusion.11), kind=kLoop, calls=%fused_computation.39.clone.1 | loop fusion | flops 8912896 | bytes 2103296 | tf_op jit(solution)/shard_map/convert
  17.9 9.0 %cosine_convert_fusion.2 = (bf16[512,1024]{1,0:T(8,128)(2,1)S(1)}, bf16[512,1024]{1,0:T(8,128)(2,1)S(1)}) fusion(s32[512]{0:T(512)S(1)} %iota_add_fusion.10, s32[1024]{0:T(1024)S(1)} %iota_add_fusion.11), kind=kLoop, calls=%fused_computation.39.clone.1 | loop fusion | flops 8912896 | bytes 2103296 | tf_op jit(solution)/shard_map/convert
  28.4 9.0 %cosine_convert_fusion.2 = (bf16[512,1024]{1,0:T(8,128)(2,1)S(1)}, bf16[512,1024]{1,0:T(8,128)(2,1)S(1)}) fusion(s32[512]{0:T(512)S(1)} %iota_add_fusion.10, s32[1024]{0:T(1024)S(1)} %iota_add_fusion.11), kind=kLoop, calls=%fused_computation.39.clone.1 | loop fusion | flops 8912896 | bytes 2103296 | tf_op jit(solution)/shard_map/convert
  39.0 9.0 %cosine_convert_fusion.2 = (bf16[512,1024]{1,0:T(8,128)(2,1)S(1)}, bf16[512,1024]{1,0:T(8,128)(2,1)S(1)}) fusion(s32[512]{0:T(512)S(1)} %iota_add_fusion.10, s32[1024]{0:T(1024)S(1)} %iota_add_fusion.11), kind=kLoop, calls=%fused_computation.39.clone.1 | loop fusion | flops 8912896 | bytes 2103296 | tf_op jit(solution)/shard_map/convert
  49.6 9.0 %cosine_convert_fusion.2 = (bf16[512,1024]{1,0:T(8,128)(2,1)S(1)}, bf16[512,1024]{1,0:T(8,128)(2,1)S(1)}) fusion(s32[512]{0:T(512)S(1)} %iota_add_fusion.10, s32[1024]{0:T(1024)S(1)} %iota_add_fusion.11), kind=kLoop, calls=%fused_computation.39.clone.1 | loop fusion | flops 8912896 | bytes 2103296 | tf_op jit(solution)/shard_map/convert
  60.2 9.0 %cosine_convert_fusion.2 = (bf16[512,1024]{1,0:T(8,128)(2,1)S(1)}, bf16[512,1024]{1,0:T(8,128)(2,1)S(1)}) fusion(s32[512]{0:T(512)S(1)} %iota_add_fusion.10, s32[1024]{0:T(1024)S(1)} %iota_add_fusion.11), kind=kLoop, calls=%fused_computation.39.clone.1 | loop fusion | flops 8912896 | bytes 2103296 | tf_op jit(solution)/shard_map/convert
  70.8 9.0 %cosine_convert_fusion.2 = (bf16[512,1024]{1,0:T(8,128)(2,1)S(1)}, bf16[512,1024]{1,0:T(8,128)(2,1)S(1)}) fusion(s32[512]{0:T(512)S(1)} %iota_add_fusion.10, s32[1024]{0:T(1024)S(1)} %iota_add_fusion.11), kind=kLoop, calls=%fused_computation.39.clone.1 | loop fusion | flops 8912896 | bytes 2103296 | tf_op jit(solution)/shard_map/convert
  81.4 9.0 %cosine_convert_fusion.2 = (bf16[512,1024]{1,0:T(8,128)(2,1)S(1)}, bf16[512,1024]{1,0:T(8,128)(2,1)S(1)}) fusion(s32[512]{0:T(512)S(1)} %iota_add_fusion.10, s32[1024]{0:T(1024)S(1)} %iota_add_fusion.11), kind=kLoop, calls=%fused_computation.39.clone.1 | loop fusion | flops 8912896 | bytes 2103296 | tf_op jit(solution)/shard_map/convert
  95.7 22.1 %all_to_all.20 = s32[64,1,4]{2,1,0:T(1,128)S(1)} all-to-all(s32[64,1,4]{2,1,0:T(1,128)S(1)} %bitcast.27), channel_id=1, replica_groups=mesh['chan'=64,'src'=4] {'chan'}, dimensions={0} | all-to-all | bytes 2048 | tf_op jit(solution)/shard_map/all_to_all | solution.py:130
  122.5 3.6 select_select_fusion
  126.1 5.7 %all-to-all-start.1 = ((f32[64,4,2048]{2,1,0:T(4,128)}), f32[64,4,2048]{2,1,0:T(4,128)}, u32[]{:S(2)}, u32[]{:S(2)}) async-start(f32[64,4,2048]{2,1,0:T(4,128)} %select_select_fusion), calls=%async_computation.1 | async-start | bytes 4194304 | tf_op jit(solution)/shard_map/all_to_all | solution.py:118
  131.9 65.0 %all-to-all-done.1 = f32[64,4,2048]{2,1,0:T(4,128)} async-done(((f32[64,4,2048]{2,1,0:T(4,128)}), f32[64,4,2048]{2,1,0:T(4,128)}, u32[]{:S(2)}, u32[]{:S(2)}) %all-to-all-start.1) | async-done | bytes 2097184 | tf_op jit(solution)/shard_map/all_to_all | solution.py:118
  199.9 3.5 all-gather.2.cloned.1.call-done
  203.3 3.8 reduce_sum.41
  213.5 8.2 %all-to-all-start.2 = ((f32[64,4,2048]{2,1,0:T(4,128)}), f32[64,4,2048]{2,1,0:T(4,128)S(1)}, u32[]{:S(2)}, u32[]{:S(2)}) async-start(f32[64,4,2048]{2,1,0:T(4,128)} %reshape.151), calls=%async_computation.2 | async-start | bytes 4194304 | tf_op jit(solution)/shard_map/all_to_all | solution.py:129
  221.9 51.1 %all-to-all-done.2 = f32[64,4,2048]{2,1,0:T(4,128)S(1)} async-done(((f32[64,4,2048]{2,1,0:T(4,128)}), f32[64,4,2048]{2,1,0:T(4,128)S(1)}, u32[]{:S(2)}, u32[]{:S(2)}) %all-to-all-start.2) | async-done | bytes 2097184 | tf_op jit(solution)/shard_map/all_to_all | solution.py:129
  278.8 101.1 %while.31 = (s32[]{:T(128)}, f32[128,4096]{1,0:T(8,128)}, f32[128,2048]{1,0:T(8,128)S(1)}, s32[]{:T(128)}, s32[]{:T(128)}, /*index=5*/s32[]{:T(128)}, s32[]{:T(128)}) while((s32[]{:T(128)}, f32[128,4096]{1,0:T(8,128)}, f32[128,2048]{1,0:T(8,128)S(1)}, s32[]{:T(128)}, s32[]{:T(128)}, /*index=5*/s32[]{:T(128)}, s32[]{:T(128)}) %tuple.90), condition=%wide.region_9.10_spmd, body=%wide.region_8.9_spmd.sunk | while | flops 1619592704 | bytes 10760323 | solution.py:52
  278.8 8.3 %fusion.47 = (f32[512,1024]{1,0:T(8,128)S(1)}, f32[512,1024]{1,0:T(8,128)S(1)}) fusion(s32[512]{0:T(512)S(1)} %iota_add_fusion.8, s32[1024]{0:T(1024)S(1)} %iota_add_fusion.9), kind=kLoop, calls=%fused_computation.21.clone.1 | loop fusion | flops 7864320 | bytes 4200448 | tf_op jit(solution)/shard_map/while/body/eval_jaxpr/cos | solution.py:15
  287.1 3.4 fusion.48
  291.5 8.3 %fusion.47 = (f32[512,1024]{1,0:T(8,128)S(1)}, f32[512,1024]{1,0:T(8,128)S(1)}) fusion(s32[512]{0:T(512)S(1)} %iota_add_fusion.8, s32[1024]{0:T(1024)S(1)} %iota_add_fusion.9), kind=kLoop, calls=%fused_computation.21.clone.1 | loop fusion | flops 7864320 | bytes 4200448 | tf_op jit(solution)/shard_map/while/body/eval_jaxpr/cos | solution.py:15
  299.8 3.4 fusion.48
  304.1 8.3 %fusion.47 = (f32[512,1024]{1,0:T(8,128)S(1)}, f32[512,1024]{1,0:T(8,128)S(1)}) fusion(s32[512]{0:T(512)S(1)} %iota_add_fusion.8, s32[1024]{0:T(1024)S(1)} %iota_add_fusion.9), kind=kLoop, calls=%fused_computation.21.clone.1 | loop fusion | flops 7864320 | bytes 4200448 | tf_op jit(solution)/shard_map/while/body/eval_jaxpr/cos | solution.py:15
  316.7 8.3 %fusion.47 = (f32[512,1024]{1,0:T(8,128)S(1)}, f32[512,1024]{1,0:T(8,128)S(1)}) fusion(s32[512]{0:T(512)S(1)} %iota_add_fusion.8, s32[1024]{0:T(1024)S(1)} %iota_add_fusion.9), kind=kLoop, calls=%fused_computation.21.clone.1 | loop fusion | flops 7864320 | bytes 4200448 | tf_op jit(solution)/shard_map/while/body/eval_jaxpr/cos | solution.py:15
  325.0 3.4 fusion.48
  329.4 8.3 %fusion.47 = (f32[512,1024]{1,0:T(8,128)S(1)}, f32[512,1024]{1,0:T(8,128)S(1)}) fusion(s32[512]{0:T(512)S(1)} %iota_add_fusion.8, s32[1024]{0:T(1024)S(1)} %iota_add_fusion.9), kind=kLoop, calls=%fused_computation.21.clone.1 | loop fusion | flops 7864320 | bytes 4200448 | tf_op jit(solution)/shard_map/while/body/eval_jaxpr/cos | solution.py:15
  337.7 3.4 fusion.48
  342.0 8.3 %fusion.47 = (f32[512,1024]{1,0:T(8,128)S(1)}, f32[512,1024]{1,0:T(8,128)S(1)}) fusion(s32[512]{0:T(512)S(1)} %iota_add_fusion.8, s32[1024]{0:T(1024)S(1)} %iota_add_fusion.9), kind=kLoop, calls=%fused_computation.21.clone.1 | loop fusion | flops 7864320 | bytes 4200448 | tf_op jit(solution)/shard_map/while/body/eval_jaxpr/cos | solution.py:15
  354.7 8.3 %fusion.47 = (f32[512,1024]{1,0:T(8,128)S(1)}, f32[512,1024]{1,0:T(8,128)S(1)}) fusion(s32[512]{0:T(512)S(1)} %iota_add_fusion.8, s32[1024]{0:T(1024)S(1)} %iota_add_fusion.9), kind=kLoop, calls=%fused_computation.21.clone.1 | loop fusion | flops 7864320 | bytes 4200448 | tf_op jit(solution)/shard_map/while/body/eval_jaxpr/cos | solution.py:15
  363.0 3.4 fusion.48
  367.3 8.3 %fusion.47 = (f32[512,1024]{1,0:T(8,128)S(1)}, f32[512,1024]{1,0:T(8,128)S(1)}) fusion(s32[512]{0:T(512)S(1)} %iota_add_fusion.8, s32[1024]{0:T(1024)S(1)} %iota_add_fusion.9), kind=kLoop, calls=%fused_computation.21.clone.1 | loop fusion | flops 7864320 | bytes 4200448 | tf_op jit(solution)/shard_map/while/body/eval_jaxpr/cos | solution.py:15
  380.4 28.6 %reduce-scatter.2.cloned.1.call-done = f32[32,4096]{1,0:T(8,128)} async-done(((f32[128,4096]{1,0:T(8,128)}), f32[32,4096]{1,0:T(8,128)}) %reduce-scatter.2.cloned.1.call-update) | async-done | bytes 524304 | tf_op jit(solution)/shard_map/reduce_scatter | solution.py:140
  (114 shorter events, 53.7 us)
Async XLA Ops:
  7.2 196.2 %all-gather.2.cloned.1.call-start = ((), (), s32[]{:S(2)}) async-start(), calls=%async_computation.4 | async-start | bytes 8519680 | tf_op jit(solution)/shard_map/all_gather | solution.py:102
  91.9 0.7 copy-start.2
  92.1 1.9 copy-start.1
  126.1 5.8 %copy-start.3 = (s32[128]{0:T(128)S(1)}, s32[128]{0:T(128)}, u32[]{:S(2)}) copy-start(s32[128]{0:T(128)} %param.14) | copy-start | bytes 1540
  126.1 70.8 %all-to-all-start.1 = ((f32[64,4,2048]{2,1,0:T(4,128)}), f32[64,4,2048]{2,1,0:T(4,128)}, u32[]{:S(2)}, u32[]{:S(2)}) async-start(f32[64,4,2048]{2,1,0:T(4,128)} %select_select_fusion), calls=%async_computation.1 | async-start | bytes 4194304 | tf_op jit(solution)/shard_map/all_to_all | solution.py:118
  208.1 1.2 copy-start
  213.5 59.5 %all-to-all-start.2 = ((f32[64,4,2048]{2,1,0:T(4,128)}), f32[64,4,2048]{2,1,0:T(4,128)S(1)}, u32[]{:S(2)}, u32[]{:S(2)}) async-start(f32[64,4,2048]{2,1,0:T(4,128)} %reshape.151), calls=%async_computation.2 | async-start | bytes 4194304 | tf_op jit(solution)/shard_map/all_to_all | solution.py:129
  221.7 187.3 %reduce-scatter.2.cloned.1.call-start = ((), (), s32[]{:S(2)}) async-start(), calls=%async_computation.5 | async-start | bytes 2621440 | tf_op jit(solution)/shard_map/reduce_scatter | solution.py:140
Sparse Core Ops, SparseCore 0:
  94.1 109.2 all-gather.1
  380.0 28.9 reduce-scatter.1
